TPU v7x, 256 devices: a whole 4x4x8 slice. The times are simulated.
256 devices in a mesh: section: 16 (over y, x), expert: 16 (over z, core).
Axes of the slice: x: 4, y: 4, z: 8, core: 2. Of those that a mesh axis runs over, the one named last changes fastest.
Arguments:
- layer_inputs: bfloat16 [16, 16, 128, 4096], P('section', None, 'expert'), may hold values from -6 to 6
- expert_ids: int32 [16, 16, 128, 2], P('section', None, 'expert'), may hold values from 0 to 7, all different within a row; in each aligned block of 8 rows (0 to 7, 8 to 15, ..., all dimensions but the last counted through in order) at most 3 rows name the same one
- gates: bfloat16 [16, 16, 128, 2], P('section', None, 'expert'), may hold values from 0.099609375 to 0.59765625
- w_gate: bfloat16 [16, 4096, 4096], P('section', None, 'expert'), may hold values from -0.09375 to 0.09375
- w_up: bfloat16 [16, 4096, 4096], P('section', None, 'expert'), may hold values from -0.09375 to 0.09375
- w_down: bfloat16 [16, 4096, 4096], P('section', 'expert'), may hold values from -0.25 to 0.25
- out_grad: bfloat16 [16, 128, 4096], P(None, 'expert'), may hold values from -6 to 6
Outputs:
- section_grads: bfloat16 [16, 16, 128, 4096], P('section', None, 'expert')
Inputs may be any that keep to these rules, and one draw needn't show every extreme that they name: `expert_ids`: within one micro-batch of one section, the 8 tokens of one expert index name each expert at most 3 times, and in some such groups one expert exactly 3 times; a token's 2 experts differ.
All inputs are finite; a program needn't handle non-finite values.
Results may differ from a plain program's by a relative error of at most 0.035.
Values may be sent and summed in bfloat16 or wider, within the bound.
A program may use at most 64 MiB of HBM per device.

v0:
```python
import jax
import jax.numpy as jnp
from jax import lax
from jax.sharding import PartitionSpec as P

EXPERTS = 8
CAP = 3


def passed_along(x, axis, by):
    length = lax.axis_size(axis)
    pairs = [(i, i + by) for i in range(length) if 0 <= i + by < length]
    return lax.ppermute(x, axis, pairs)


def selection(choices, capacity):
    token_count, top_count = (choices.shape[-2], choices.shape[-1])
    experts = jnp.arange(EXPERTS, dtype=jnp.int32)
    onehot = (choices[..., None] == experts).astype(jnp.int32)
    leading = onehot.shape[:-3]
    flattened = onehot.reshape(leading + (token_count * top_count, EXPERTS))
    before = jnp.cumsum(flattened, axis=-2) - flattened
    slot_index = jnp.sum((before * flattened).reshape(onehot.shape), axis=-1)
    places = jnp.arange(capacity, dtype=jnp.int32)
    in_slot = (slot_index[..., None] == places).astype(jnp.int32)
    return onehot[..., None] * in_slot[..., None, :]


def on_device(layer_inputs, expert_ids, gates, w_gate, w_up, w_down, out_grad):
    expert_count = lax.axis_size("expert")
    section_count = lax.axis_size("section")
    section_index = lax.axis_index("section")
    inputs = layer_inputs[0]
    gate_slice = w_gate[0]
    up_slice = w_up[0]
    down_slice = w_down[0]
    micro_count, token_count, model_width = inputs.shape
    hidden = gate_slice.shape[1]
    shards = expert_count // EXPERTS
    capacity = CAP
    slot_rows = expert_count * capacity
    contract = (((1,), (1,)), ((), ()))
    selected = selection(expert_ids[0], capacity)
    dispatch = jnp.sum(selected, axis=2).astype(jnp.bfloat16)
    gate_values = gates[0].astype(jnp.float32)
    combine = jnp.sum(selected.astype(jnp.float32) * gate_values[..., None, None], axis=2).astype(
        jnp.bfloat16
    )

    def spread(rows):
        leading = rows.shape[:-3]
        rows = rows.astype(jnp.bfloat16)
        rows = jnp.broadcast_to(
            jnp.expand_dims(rows, -3), leading + (EXPERTS, shards, capacity, model_width)
        )
        return rows.reshape(leading + (expert_count, capacity, model_width))

    def backward_rows(grad_block, act, coef):
        down_grad = lax.dot_general(
            grad_block, down_slice, contract, preferred_element_type=jnp.float32
        )
        dgate = (down_grad * coef).astype(jnp.bfloat16)
        dup = (down_grad * act).astype(jnp.bfloat16)
        total = lax.dot_general(dgate, gate_slice, contract, preferred_element_type=jnp.float32)
        total = total + lax.dot_general(dup, up_slice, contract, preferred_element_type=jnp.float32)
        return total.astype(jnp.bfloat16)

    zeros_back = jnp.zeros((slot_rows, model_width), jnp.bfloat16)
    outgoing = spread(
        jnp.einsum("mtec,mtd->mecd", dispatch, inputs, preferred_element_type=jnp.float32)
    )
    received = lax.all_to_all(outgoing, "expert", split_axis=1, concat_axis=1, tiled=True)
    item_count = received.shape[0]
    row_block = received.reshape(-1, model_width)
    pre_gate = jnp.dot(row_block, gate_slice, preferred_element_type=jnp.float32)
    pre_up = jnp.dot(row_block, up_slice, preferred_element_type=jnp.float32)
    sigmoid_gate = jax.nn.sigmoid(pre_gate)
    act = pre_gate * sigmoid_gate
    coef = pre_up * (sigmoid_gate * (1.0 + pre_gate * (1.0 - sigmoid_gate)))
    act, coef = (act, coef)
    saved = jnp.stack([act, coef]).reshape(2, item_count, slot_rows, hidden)
    act_all = saved[0]
    coef_all = saved[1]

    def tick(tick_index, state_pair):
        incoming, results = state_pair
        micro_index = tick_index - (section_count - 1 - section_index)
        active = (micro_index >= 0) & (micro_index < micro_count)
        micro_slot = jnp.clip(micro_index, 0, micro_count - 1)
        top_grad = lax.dynamic_index_in_dim(out_grad, micro_slot, 0, keepdims=False)
        grad_out = jnp.where(section_index == section_count - 1, top_grad, incoming)
        dispatch_micro = lax.dynamic_index_in_dim(dispatch, micro_slot, 0, keepdims=False)
        combine_micro = lax.dynamic_index_in_dim(combine, micro_slot, 0, keepdims=False)
        grad_rows = spread(
            jnp.einsum("tec,td->ecd", dispatch_micro, grad_out, preferred_element_type=jnp.float32)
        )
        arrived = lax.all_to_all(
            grad_rows, "expert", split_axis=0, concat_axis=0, tiled=True
        ).reshape(slot_rows, model_width)

        def local_saved(row_block):
            act = lax.dynamic_index_in_dim(act_all, micro_slot, 0, keepdims=False)
            coef = lax.dynamic_index_in_dim(coef_all, micro_slot, 0, keepdims=False)
            return backward_rows(row_block, act, coef)

        def skip_saved(row_block):
            return zeros_back

        back = lax.cond(active, local_saved, skip_saved, arrived)
        returned = lax.all_to_all(
            back.reshape(expert_count, capacity, model_width),
            "expert",
            split_axis=0,
            concat_axis=0,
            tiled=True,
        )
        returned = returned.reshape(EXPERTS, shards, capacity, model_width)
        mixed = jnp.einsum(
            "tec,ekcd->td", combine_micro, returned, preferred_element_type=jnp.float32
        )
        grad_in = (grad_out.astype(jnp.float32) + mixed).astype(jnp.bfloat16)
        updated = lax.dynamic_update_index_in_dim(results, grad_in, micro_slot, 0)
        results = jnp.where(active, updated, results)
        passed = passed_along(grad_in, "section", -1)
        return (passed, results)

    initial = (
        jnp.zeros((token_count, model_width), jnp.bfloat16),
        jnp.zeros((micro_count, token_count, model_width), jnp.bfloat16),
    )
    final_state = lax.fori_loop(0, micro_count + section_count - 1, tick, initial)
    return final_state[1][None]


def solution(mesh):
    placed = (
        P("section", None, "expert", None),
        P("section", None, "expert", None),
        P("section", None, "expert", None),
        P("section", None, "expert"),
        P("section", None, "expert"),
        P("section", "expert", None),
        P(None, "expert", None),
    )
    return jax.shard_map(
        on_device,
        mesh=mesh,
        in_specs=placed,
        out_specs=P("section", None, "expert", None),
        check_vma=False,
    )
```

profile of v0, /device:TPU:1, one launch (start us, length us, event | category | flops | bytes accessed | tf_op | source)
XLA Modules:
  0.0 2030.5 jit_solution(850015349437797174)
XLA Ops:
  19.4 137.7 %all-to-all-done.2 = bf16[16,16,3,4096]{3,0,2,1:T(8,128)(2,1)} async-done(((bf16[16,16,3,4096]{3,0,2,1:T(8,128)(2,1)}), bf16[16,16,3,4096]{3,0,2,1:T(8,128)(2,1)}, u32[]{:S(2)}, u32[]{:S(2)}) %all-to-all-start.2) | async-done | bytes 6291488 | tf_op jit(solution)/shard_map/all_to_all | solution.py:72
  191.9 1838.6 %while.17 = (s32[]{:T(128)}, bf16[8,4096]{1,0:T(8,128)(2,1)S(1)}, bf16[16,8,4096]{2,1,0:T(8,128)(2,1)}, pred[]{:T(512)}, s32[]{:T(128)}, /*index=5*/bf16[16,8,40...) while((s32[]{:T(128)}, bf16[8,4096]{1,0:T(8,128)(2,1)S(1)}, ...), condition=%wide.region_8.9_spmd, body=%wide.region_4.8_spmd.sunk | while | flops 306167808 | bytes 32488984 | solution.py:131
  200.0 17.4 all-to-all-done
  218.5 20.3 all_to_all.29
  252.5 17.5 all-to-all-done
  271.1 20.3 %all_to_all.29 = bf16[16,3,4096]{2,1,0:T(4,128)(2,1)S(1)} all-to-all(bf16[16,3,4096]{2,1,0:T(4,128)(2,1)} %reshape.87), channel_id=1, replica_groups=mesh['section'=16,'expert'=16] {'expert'}, dimensions={0} | all-to-all | bytes 786432 | tf_op jit(solution)/shard_map/while/body/eval_jaxpr/all_to_all | solution.py:110
  305.2 17.5 all-to-all-done
  323.7 20.3 %all_to_all.29 = bf16[16,3,4096]{2,1,0:T(4,128)(2,1)S(1)} all-to-all(bf16[16,3,4096]{2,1,0:T(4,128)(2,1)} %reshape.87), channel_id=1, replica_groups=mesh['section'=16,'expert'=16] {'expert'}, dimensions={0} | all-to-all | bytes 786432 | tf_op jit(solution)/shard_map/while/body/eval_jaxpr/all_to_all | solution.py:110
  357.9 17.5 all-to-all-done
  376.4 20.3 %all_to_all.29 = bf16[16,3,4096]{2,1,0:T(4,128)(2,1)S(1)} all-to-all(bf16[16,3,4096]{2,1,0:T(4,128)(2,1)} %reshape.87), channel_id=1, replica_groups=mesh['section'=16,'expert'=16] {'expert'}, dimensions={0} | all-to-all | bytes 786432 | tf_op jit(solution)/shard_map/while/body/eval_jaxpr/all_to_all | solution.py:110
  410.5 17.3 all-to-all-done
  428.9 20.3 %all_to_all.29 = bf16[16,3,4096]{2,1,0:T(4,128)(2,1)S(1)} all-to-all(bf16[16,3,4096]{2,1,0:T(4,128)(2,1)} %reshape.87), channel_id=1, replica_groups=mesh['section'=16,'expert'=16] {'expert'}, dimensions={0} | all-to-all | bytes 786432 | tf_op jit(solution)/shard_map/while/body/eval_jaxpr/all_to_all | solution.py:110
  483.4 20.3 %all_to_all.29 = bf16[16,3,4096]{2,1,0:T(4,128)(2,1)S(1)} all-to-all(bf16[16,3,4096]{2,1,0:T(4,128)(2,1)} %reshape.87), channel_id=1, replica_groups=mesh['section'=16,'expert'=16] {'expert'}, dimensions={0} | all-to-all | bytes 786432 | tf_op jit(solution)/shard_map/while/body/eval_jaxpr/all_to_all | solution.py:110
  519.9 17.2 all-to-all-done
  538.2 20.3 %all_to_all.29 = bf16[16,3,4096]{2,1,0:T(4,128)(2,1)S(1)} all-to-all(bf16[16,3,4096]{2,1,0:T(4,128)(2,1)} %reshape.87), channel_id=1, replica_groups=mesh['section'=16,'expert'=16] {'expert'}, dimensions={0} | all-to-all | bytes 786432 | tf_op jit(solution)/shard_map/while/body/eval_jaxpr/all_to_all | solution.py:110
  574.7 17.2 all-to-all-done
  593.0 20.3 %all_to_all.29 = bf16[16,3,4096]{2,1,0:T(4,128)(2,1)S(1)} all-to-all(bf16[16,3,4096]{2,1,0:T(4,128)(2,1)} %reshape.87), channel_id=1, replica_groups=mesh['section'=16,'expert'=16] {'expert'}, dimensions={0} | all-to-all | bytes 786432 | tf_op jit(solution)/shard_map/while/body/eval_jaxpr/all_to_all | solution.py:110
  629.5 17.2 all-to-all-done
  647.7 20.3 %all_to_all.29 = bf16[16,3,4096]{2,1,0:T(4,128)(2,1)S(1)} all-to-all(bf16[16,3,4096]{2,1,0:T(4,128)(2,1)} %reshape.87), channel_id=1, replica_groups=mesh['section'=16,'expert'=16] {'expert'}, dimensions={0} | all-to-all | bytes 786432 | tf_op jit(solution)/shard_map/while/body/eval_jaxpr/all_to_all | solution.py:110
  684.2 17.2 all-to-all-done
  702.5 20.3 %all_to_all.29 = bf16[16,3,4096]{2,1,0:T(4,128)(2,1)S(1)} all-to-all(bf16[16,3,4096]{2,1,0:T(4,128)(2,1)} %reshape.87), channel_id=1, replica_groups=mesh['section'=16,'expert'=16] {'expert'}, dimensions={0} | all-to-all | bytes 786432 | tf_op jit(solution)/shard_map/while/body/eval_jaxpr/all_to_all | solution.py:110
  739.0 17.2 all-to-all-done
  757.2 20.3 %all_to_all.29 = bf16[16,3,4096]{2,1,0:T(4,128)(2,1)S(1)} all-to-all(bf16[16,3,4096]{2,1,0:T(4,128)(2,1)} %reshape.87), channel_id=1, replica_groups=mesh['section'=16,'expert'=16] {'expert'}, dimensions={0} | all-to-all | bytes 786432 | tf_op jit(solution)/shard_map/while/body/eval_jaxpr/all_to_all | solution.py:110
  793.8 17.2 all-to-all-done
  812.0 20.3 %all_to_all.29 = bf16[16,3,4096]{2,1,0:T(4,128)(2,1)S(1)} all-to-all(bf16[16,3,4096]{2,1,0:T(4,128)(2,1)} %reshape.87), channel_id=1, replica_groups=mesh['section'=16,'expert'=16] {'expert'}, dimensions={0} | all-to-all | bytes 786432 | tf_op jit(solution)/shard_map/while/body/eval_jaxpr/all_to_all | solution.py:110
  848.5 17.2 all-to-all-done
  866.8 20.3 %all_to_all.29 = bf16[16,3,4096]{2,1,0:T(4,128)(2,1)S(1)} all-to-all(bf16[16,3,4096]{2,1,0:T(4,128)(2,1)} %reshape.87), channel_id=1, replica_groups=mesh['section'=16,'expert'=16] {'expert'}, dimensions={0} | all-to-all | bytes 786432 | tf_op jit(solution)/shard_map/while/body/eval_jaxpr/all_to_all | solution.py:110
  903.3 17.2 all-to-all-done
  921.5 20.3 %all_to_all.29 = bf16[16,3,4096]{2,1,0:T(4,128)(2,1)S(1)} all-to-all(bf16[16,3,4096]{2,1,0:T(4,128)(2,1)} %reshape.87), channel_id=1, replica_groups=mesh['section'=16,'expert'=16] {'expert'}, dimensions={0} | all-to-all | bytes 786432 | tf_op jit(solution)/shard_map/while/body/eval_jaxpr/all_to_all | solution.py:110
  958.0 17.2 all-to-all-done
  976.3 20.3 %all_to_all.29 = bf16[16,3,4096]{2,1,0:T(4,128)(2,1)S(1)} all-to-all(bf16[16,3,4096]{2,1,0:T(4,128)(2,1)} %reshape.87), channel_id=1, replica_groups=mesh['section'=16,'expert'=16] {'expert'}, dimensions={0} | all-to-all | bytes 786432 | tf_op jit(solution)/shard_map/while/body/eval_jaxpr/all_to_all | solution.py:110
  1000.1 60.6 %collective-permute-done = bf16[8,4096]{1,0:T(8,128)(2,1)S(1)} collective-permute-done((bf16[8,4096]{1,0:T(8,128)(2,1)S(1)}, bf16[8,4096]{1,0:T(8,128)(2,1)S(1)}, u32[]{:S(2)}, u32[]{:S(2)}) %collective-permute-start) | collective-permute-done | bytes 65568 | tf_op jit(solution)/shard_map/while/body/eval_jaxpr/ppermute | solution.py:13
  1067.1 17.2 all-to-all-done
  1091.4 20.3 %all_to_all.29 = bf16[16,3,4096]{2,1,0:T(4,128)(2,1)S(1)} all-to-all(bf16[16,3,4096]{2,1,0:T(4,128)(2,1)} %reshape.87), channel_id=1, replica_groups=mesh['section'=16,'expert'=16] {'expert'}, dimensions={0} | all-to-all | bytes 786432 | tf_op jit(solution)/shard_map/while/body/eval_jaxpr/all_to_all | solution.py:110
  1127.9 17.2 all-to-all-done
  1152.2 20.3 %all_to_all.29 = bf16[16,3,4096]{2,1,0:T(4,128)(2,1)S(1)} all-to-all(bf16[16,3,4096]{2,1,0:T(4,128)(2,1)} %reshape.87), channel_id=1, replica_groups=mesh['section'=16,'expert'=16] {'expert'}, dimensions={0} | all-to-all | bytes 786432 | tf_op jit(solution)/shard_map/while/body/eval_jaxpr/all_to_all | solution.py:110
  1188.6 17.2 all-to-all-done
  1212.9 20.3 %all_to_all.29 = bf16[16,3,4096]{2,1,0:T(4,128)(2,1)S(1)} all-to-all(bf16[16,3,4096]{2,1,0:T(4,128)(2,1)} %reshape.87), channel_id=1, replica_groups=mesh['section'=16,'expert'=16] {'expert'}, dimensions={0} | all-to-all | bytes 786432 | tf_op jit(solution)/shard_map/while/body/eval_jaxpr/all_to_all | solution.py:110
  1249.4 17.2 all-to-all-done
  1273.7 20.3 %all_to_all.29 = bf16[16,3,4096]{2,1,0:T(4,128)(2,1)S(1)} all-to-all(bf16[16,3,4096]{2,1,0:T(4,128)(2,1)} %reshape.87), channel_id=1, replica_groups=mesh['section'=16,'expert'=16] {'expert'}, dimensions={0} | all-to-all | bytes 786432 | tf_op jit(solution)/shard_map/while/body/eval_jaxpr/all_to_all | solution.py:110
  1310.2 17.2 all-to-all-done
  1334.5 20.3 %all_to_all.29 = bf16[16,3,4096]{2,1,0:T(4,128)(2,1)S(1)} all-to-all(bf16[16,3,4096]{2,1,0:T(4,128)(2,1)} %reshape.87), channel_id=1, replica_groups=mesh['section'=16,'expert'=16] {'expert'}, dimensions={0} | all-to-all | bytes 786432 | tf_op jit(solution)/shard_map/while/body/eval_jaxpr/all_to_all | solution.py:110
  1370.9 17.2 all-to-all-done
  1395.2 20.3 %all_to_all.29 = bf16[16,3,4096]{2,1,0:T(4,128)(2,1)S(1)} all-to-all(bf16[16,3,4096]{2,1,0:T(4,128)(2,1)} %reshape.87), channel_id=1, replica_groups=mesh['section'=16,'expert'=16] {'expert'}, dimensions={0} | all-to-all | bytes 786432 | tf_op jit(solution)/shard_map/while/body/eval_jaxpr/all_to_all | solution.py:110
  1431.7 17.2 all-to-all-done
  1456.0 20.3 %all_to_all.29 = bf16[16,3,4096]{2,1,0:T(4,128)(2,1)S(1)} all-to-all(bf16[16,3,4096]{2,1,0:T(4,128)(2,1)} %reshape.87), channel_id=1, replica_groups=mesh['section'=16,'expert'=16] {'expert'}, dimensions={0} | all-to-all | bytes 786432 | tf_op jit(solution)/shard_map/while/body/eval_jaxpr/all_to_all | solution.py:110
  1492.5 17.2 all-to-all-done
  1516.8 20.3 %all_to_all.29 = bf16[16,3,4096]{2,1,0:T(4,128)(2,1)S(1)} all-to-all(bf16[16,3,4096]{2,1,0:T(4,128)(2,1)} %reshape.87), channel_id=1, replica_groups=mesh['section'=16,'expert'=16] {'expert'}, dimensions={0} | all-to-all | bytes 786432 | tf_op jit(solution)/shard_map/while/body/eval_jaxpr/all_to_all | solution.py:110
  1553.2 17.2 all-to-all-done
  1577.5 20.3 %all_to_all.29 = bf16[16,3,4096]{2,1,0:T(4,128)(2,1)S(1)} all-to-all(bf16[16,3,4096]{2,1,0:T(4,128)(2,1)} %reshape.87), channel_id=1, replica_groups=mesh['section'=16,'expert'=16] {'expert'}, dimensions={0} | all-to-all | bytes 786432 | tf_op jit(solution)/shard_map/while/body/eval_jaxpr/all_to_all | solution.py:110
  1614.0 17.2 all-to-all-done
  1638.3 20.3 %all_to_all.29 = bf16[16,3,4096]{2,1,0:T(4,128)(2,1)S(1)} all-to-all(bf16[16,3,4096]{2,1,0:T(4,128)(2,1)} %reshape.87), channel_id=1, replica_groups=mesh['section'=16,'expert'=16] {'expert'}, dimensions={0} | all-to-all | bytes 786432 | tf_op jit(solution)/shard_map/while/body/eval_jaxpr/all_to_all | solution.py:110
  1674.7 17.2 all-to-all-done
  1699.0 20.3 %all_to_all.29 = bf16[16,3,4096]{2,1,0:T(4,128)(2,1)S(1)} all-to-all(bf16[16,3,4096]{2,1,0:T(4,128)(2,1)} %reshape.87), channel_id=1, replica_groups=mesh['section'=16,'expert'=16] {'expert'}, dimensions={0} | all-to-all | bytes 786432 | tf_op jit(solution)/shard_map/while/body/eval_jaxpr/all_to_all | solution.py:110
  1735.5 17.2 all-to-all-done
  1759.8 20.3 %all_to_all.29 = bf16[16,3,4096]{2,1,0:T(4,128)(2,1)S(1)} all-to-all(bf16[16,3,4096]{2,1,0:T(4,128)(2,1)} %reshape.87), channel_id=1, replica_groups=mesh['section'=16,'expert'=16] {'expert'}, dimensions={0} | all-to-all | bytes 786432 | tf_op jit(solution)/shard_map/while/body/eval_jaxpr/all_to_all | solution.py:110
  1796.3 17.2 all-to-all-done
  1820.6 20.3 %all_to_all.29 = bf16[16,3,4096]{2,1,0:T(4,128)(2,1)S(1)} all-to-all(bf16[16,3,4096]{2,1,0:T(4,128)(2,1)} %reshape.87), channel_id=1, replica_groups=mesh['section'=16,'expert'=16] {'expert'}, dimensions={0} | all-to-all | bytes 786432 | tf_op jit(solution)/shard_map/while/body/eval_jaxpr/all_to_all | solution.py:110
  1857.0 17.2 all-to-all-done
  1881.3 20.3 %all_to_all.29 = bf16[16,3,4096]{2,1,0:T(4,128)(2,1)S(1)} all-to-all(bf16[16,3,4096]{2,1,0:T(4,128)(2,1)} %reshape.87), channel_id=1, replica_groups=mesh['section'=16,'expert'=16] {'expert'}, dimensions={0} | all-to-all | bytes 786432 | tf_op jit(solution)/shard_map/while/body/eval_jaxpr/all_to_all | solution.py:110
  1917.8 17.2 all-to-all-done
  1942.1 20.3 %all_to_all.29 = bf16[16,3,4096]{2,1,0:T(4,128)(2,1)S(1)} all-to-all(bf16[16,3,4096]{2,1,0:T(4,128)(2,1)} %reshape.87), channel_id=1, replica_groups=mesh['section'=16,'expert'=16] {'expert'}, dimensions={0} | all-to-all | bytes 786432 | tf_op jit(solution)/shard_map/while/body/eval_jaxpr/all_to_all | solution.py:110
  1978.6 17.2 all-to-all-done
  2002.9 20.3 %all_to_all.29 = bf16[16,3,4096]{2,1,0:T(4,128)(2,1)S(1)} all-to-all(bf16[16,3,4096]{2,1,0:T(4,128)(2,1)} %reshape.87), channel_id=1, replica_groups=mesh['section'=16,'expert'=16] {'expert'}, dimensions={0} | all-to-all | bytes 786432 | tf_op jit(solution)/shard_map/while/body/eval_jaxpr/all_to_all | solution.py:110
  (670 shorter events, 779.3 us)
Async XLA Ops:
  8.5 148.7 %all-to-all-start.2 = ((bf16[16,16,3,4096]{3,0,2,1:T(8,128)(2,1)}), bf16[16,16,3,4096]{3,0,2,1:T(8,128)(2,1)}, u32[]{:S(2)}, u32[]{:S(2)}) async-start(bf16[16,16,3,4096]{3,0,2,1:T(8,128)(2,1)} %bitcast.92), calls=%async_computation.2 | async-start | bytes 12582912 | tf_op jit(solution)/shard_map/all_to_all | solution.py:72
  194.5 22.9 %all-to-all-start = ((bf16[16,3,4096]{2,1,0:T(4,128)(2,1)}), bf16[16,3,4096]{2,1,0:T(4,128)(2,1)}, u32[]{:S(2)}, u32[]{:S(2)}) async-start(bf16[16,3,4096]{2,1,0:T(4,128)(2,1)} %bitcast.91), calls=%async_computation | async-start | bytes 1048576 | tf_op jit(solution)/shard_map/while/body/eval_jaxpr/all_to_all | solution.py:97
  240.9 5.2 collective-permute-start
  248.4 21.6 %all-to-all-start = ((bf16[16,3,4096]{2,1,0:T(4,128)(2,1)}), bf16[16,3,4096]{2,1,0:T(4,128)(2,1)}, u32[]{:S(2)}, u32[]{:S(2)}) async-start(bf16[16,3,4096]{2,1,0:T(4,128)(2,1)} %bitcast.91), calls=%async_computation | async-start | bytes 1048576 | tf_op jit(solution)/shard_map/while/body/eval_jaxpr/all_to_all | solution.py:97
  293.5 5.2 collective-permute-start
  301.0 21.7 %all-to-all-start = ((bf16[16,3,4096]{2,1,0:T(4,128)(2,1)}), bf16[16,3,4096]{2,1,0:T(4,128)(2,1)}, u32[]{:S(2)}, u32[]{:S(2)}) async-start(bf16[16,3,4096]{2,1,0:T(4,128)(2,1)} %bitcast.91), calls=%async_computation | async-start | bytes 1048576 | tf_op jit(solution)/shard_map/while/body/eval_jaxpr/all_to_all | solution.py:97
  346.2 5.2 collective-permute-start
  353.6 21.7 %all-to-all-start = ((bf16[16,3,4096]{2,1,0:T(4,128)(2,1)}), bf16[16,3,4096]{2,1,0:T(4,128)(2,1)}, u32[]{:S(2)}, u32[]{:S(2)}) async-start(bf16[16,3,4096]{2,1,0:T(4,128)(2,1)} %bitcast.91), calls=%async_computation | async-start | bytes 1048576 | tf_op jit(solution)/shard_map/while/body/eval_jaxpr/all_to_all | solution.py:97
  398.8 5.2 collective-permute-start
  406.3 21.5 %all-to-all-start = ((bf16[16,3,4096]{2,1,0:T(4,128)(2,1)}), bf16[16,3,4096]{2,1,0:T(4,128)(2,1)}, u32[]{:S(2)}, u32[]{:S(2)}) async-start(bf16[16,3,4096]{2,1,0:T(4,128)(2,1)} %bitcast.91), calls=%async_computation | async-start | bytes 1048576 | tf_op jit(solution)/shard_map/while/body/eval_jaxpr/all_to_all | solution.py:97
  451.3 7.4 collective-permute-start
  461.0 21.3 %all-to-all-start = ((bf16[16,3,4096]{2,1,0:T(4,128)(2,1)}), bf16[16,3,4096]{2,1,0:T(4,128)(2,1)}, u32[]{:S(2)}, u32[]{:S(2)}) async-start(bf16[16,3,4096]{2,1,0:T(4,128)(2,1)} %bitcast.91), calls=%async_computation | async-start | bytes 1048576 | tf_op jit(solution)/shard_map/while/body/eval_jaxpr/all_to_all | solution.py:97
  505.9 7.6 collective-permute-start
  515.8 21.3 %all-to-all-start = ((bf16[16,3,4096]{2,1,0:T(4,128)(2,1)}), bf16[16,3,4096]{2,1,0:T(4,128)(2,1)}, u32[]{:S(2)}, u32[]{:S(2)}) async-start(bf16[16,3,4096]{2,1,0:T(4,128)(2,1)} %bitcast.91), calls=%async_computation | async-start | bytes 1048576 | tf_op jit(solution)/shard_map/while/body/eval_jaxpr/all_to_all | solution.py:97
  560.7 7.6 collective-permute-start
  570.5 21.3 %all-to-all-start = ((bf16[16,3,4096]{2,1,0:T(4,128)(2,1)}), bf16[16,3,4096]{2,1,0:T(4,128)(2,1)}, u32[]{:S(2)}, u32[]{:S(2)}) async-start(bf16[16,3,4096]{2,1,0:T(4,128)(2,1)} %bitcast.91), calls=%async_computation | async-start | bytes 1048576 | tf_op jit(solution)/shard_map/while/body/eval_jaxpr/all_to_all | solution.py:97
  615.4 7.6 collective-permute-start
  625.3 21.3 %all-to-all-start = ((bf16[16,3,4096]{2,1,0:T(4,128)(2,1)}), bf16[16,3,4096]{2,1,0:T(4,128)(2,1)}, u32[]{:S(2)}, u32[]{:S(2)}) async-start(bf16[16,3,4096]{2,1,0:T(4,128)(2,1)} %bitcast.91), calls=%async_computation | async-start | bytes 1048576 | tf_op jit(solution)/shard_map/while/body/eval_jaxpr/all_to_all | solution.py:97
  670.2 7.6 collective-permute-start
  680.1 21.3 %all-to-all-start = ((bf16[16,3,4096]{2,1,0:T(4,128)(2,1)}), bf16[16,3,4096]{2,1,0:T(4,128)(2,1)}, u32[]{:S(2)}, u32[]{:S(2)}) async-start(bf16[16,3,4096]{2,1,0:T(4,128)(2,1)} %bitcast.91), calls=%async_computation | async-start | bytes 1048576 | tf_op jit(solution)/shard_map/while/body/eval_jaxpr/all_to_all | solution.py:97
  725.0 7.6 collective-permute-start
  734.8 21.3 %all-to-all-start = ((bf16[16,3,4096]{2,1,0:T(4,128)(2,1)}), bf16[16,3,4096]{2,1,0:T(4,128)(2,1)}, u32[]{:S(2)}, u32[]{:S(2)}) async-start(bf16[16,3,4096]{2,1,0:T(4,128)(2,1)} %bitcast.91), calls=%async_computation | async-start | bytes 1048576 | tf_op jit(solution)/shard_map/while/body/eval_jaxpr/all_to_all | solution.py:97
  779.7 7.6 collective-permute-start
  789.6 21.3 %all-to-all-start = ((bf16[16,3,4096]{2,1,0:T(4,128)(2,1)}), bf16[16,3,4096]{2,1,0:T(4,128)(2,1)}, u32[]{:S(2)}, u32[]{:S(2)}) async-start(bf16[16,3,4096]{2,1,0:T(4,128)(2,1)} %bitcast.91), calls=%async_computation | async-start | bytes 1048576 | tf_op jit(solution)/shard_map/while/body/eval_jaxpr/all_to_all | solution.py:97
  834.5 7.6 collective-permute-start
  844.4 21.3 %all-to-all-start = ((bf16[16,3,4096]{2,1,0:T(4,128)(2,1)}), bf16[16,3,4096]{2,1,0:T(4,128)(2,1)}, u32[]{:S(2)}, u32[]{:S(2)}) async-start(bf16[16,3,4096]{2,1,0:T(4,128)(2,1)} %bitcast.91), calls=%async_computation | async-start | bytes 1048576 | tf_op jit(solution)/shard_map/while/body/eval_jaxpr/all_to_all | solution.py:97
  889.3 7.6 collective-permute-start
  899.1 21.3 %all-to-all-start = ((bf16[16,3,4096]{2,1,0:T(4,128)(2,1)}), bf16[16,3,4096]{2,1,0:T(4,128)(2,1)}, u32[]{:S(2)}, u32[]{:S(2)}) async-start(bf16[16,3,4096]{2,1,0:T(4,128)(2,1)} %bitcast.91), calls=%async_computation | async-start | bytes 1048576 | tf_op jit(solution)/shard_map/while/body/eval_jaxpr/all_to_all | solution.py:97
  944.0 7.6 collective-permute-start
  953.9 21.3 %all-to-all-start = ((bf16[16,3,4096]{2,1,0:T(4,128)(2,1)}), bf16[16,3,4096]{2,1,0:T(4,128)(2,1)}, u32[]{:S(2)}, u32[]{:S(2)}) async-start(bf16[16,3,4096]{2,1,0:T(4,128)(2,1)} %bitcast.91), calls=%async_computation | async-start | bytes 1048576 | tf_op jit(solution)/shard_map/while/body/eval_jaxpr/all_to_all | solution.py:97
  976.3 84.3 %copy-start.9 = (bf16[16,8,8,3]{1,2,3,0:T(8,128)(2,1)S(1)}, bf16[16,8,8,3]{1,2,3,0:T(8,128)(2,1)}, u32[]{:S(2)}) copy-start(bf16[16,8,8,3]{1,2,3,0:T(8,128)(2,1)} %copy-done.8) | copy-start | bytes 18436 | tf_op jit(solution)/shard_map/while
  998.8 61.9 %collective-permute-start = (bf16[8,4096]{1,0:T(8,128)(2,1)S(1)}, bf16[8,4096]{1,0:T(8,128)(2,1)S(1)}, u32[]{:S(2)}, u32[]{:S(2)}) collective-permute-start(bf16[8,4096]{1,0:T(8,128)(2,1)S(1)} %get-tuple-element.441), channel_id=1, source_target_pairs={{16,0},{32,16},{48,32},{64,48},{80,64},{96,80},{112,96},{128,112},... | collective-permute-start | bytes 196616 | tf_op jit(solution)/shard_map/while/body/eval_jaxpr/ppermute | solution.py:13
  1062.9 21.4 %all-to-all-start = ((bf16[16,3,4096]{2,1,0:T(4,128)(2,1)}), bf16[16,3,4096]{2,1,0:T(4,128)(2,1)}, u32[]{:S(2)}, u32[]{:S(2)}) async-start(bf16[16,3,4096]{2,1,0:T(4,128)(2,1)} %bitcast.91), calls=%async_computation | async-start | bytes 1048576 | tf_op jit(solution)/shard_map/while/body/eval_jaxpr/all_to_all | solution.py:97
  1113.8 7.6 collective-permute-start
  1123.7 21.4 %all-to-all-start = ((bf16[16,3,4096]{2,1,0:T(4,128)(2,1)}), bf16[16,3,4096]{2,1,0:T(4,128)(2,1)}, u32[]{:S(2)}, u32[]{:S(2)}) async-start(bf16[16,3,4096]{2,1,0:T(4,128)(2,1)} %bitcast.91), calls=%async_computation | async-start | bytes 1048576 | tf_op jit(solution)/shard_map/while/body/eval_jaxpr/all_to_all | solution.py:97
  1174.6 7.5 collective-permute-start
  1184.4 21.4 %all-to-all-start = ((bf16[16,3,4096]{2,1,0:T(4,128)(2,1)}), bf16[16,3,4096]{2,1,0:T(4,128)(2,1)}, u32[]{:S(2)}, u32[]{:S(2)}) async-start(bf16[16,3,4096]{2,1,0:T(4,128)(2,1)} %bitcast.91), calls=%async_computation | async-start | bytes 1048576 | tf_op jit(solution)/shard_map/while/body/eval_jaxpr/all_to_all | solution.py:97
  1235.4 7.6 collective-permute-start
  1245.2 21.4 %all-to-all-start = ((bf16[16,3,4096]{2,1,0:T(4,128)(2,1)}), bf16[16,3,4096]{2,1,0:T(4,128)(2,1)}, u32[]{:S(2)}, u32[]{:S(2)}) async-start(bf16[16,3,4096]{2,1,0:T(4,128)(2,1)} %bitcast.91), calls=%async_computation | async-start | bytes 1048576 | tf_op jit(solution)/shard_map/while/body/eval_jaxpr/all_to_all | solution.py:97
  1296.1 7.6 collective-permute-start
  1306.0 21.4 %all-to-all-start = ((bf16[16,3,4096]{2,1,0:T(4,128)(2,1)}), bf16[16,3,4096]{2,1,0:T(4,128)(2,1)}, u32[]{:S(2)}, u32[]{:S(2)}) async-start(bf16[16,3,4096]{2,1,0:T(4,128)(2,1)} %bitcast.91), calls=%async_computation | async-start | bytes 1048576 | tf_op jit(solution)/shard_map/while/body/eval_jaxpr/all_to_all | solution.py:97
  1356.9 7.5 collective-permute-start
  1366.7 21.4 %all-to-all-start = ((bf16[16,3,4096]{2,1,0:T(4,128)(2,1)}), bf16[16,3,4096]{2,1,0:T(4,128)(2,1)}, u32[]{:S(2)}, u32[]{:S(2)}) async-start(bf16[16,3,4096]{2,1,0:T(4,128)(2,1)} %bitcast.91), calls=%async_computation | async-start | bytes 1048576 | tf_op jit(solution)/shard_map/while/body/eval_jaxpr/all_to_all | solution.py:97
  1417.7 7.6 collective-permute-start
  1427.6 21.4 %all-to-all-start = ((bf16[16,3,4096]{2,1,0:T(4,128)(2,1)}), bf16[16,3,4096]{2,1,0:T(4,128)(2,1)}, u32[]{:S(2)}, u32[]{:S(2)}) async-start(bf16[16,3,4096]{2,1,0:T(4,128)(2,1)} %bitcast.91), calls=%async_computation | async-start | bytes 1048576 | tf_op jit(solution)/shard_map/while/body/eval_jaxpr/all_to_all | solution.py:97
  1478.5 7.6 collective-permute-start
  1488.3 21.4 %all-to-all-start = ((bf16[16,3,4096]{2,1,0:T(4,128)(2,1)}), bf16[16,3,4096]{2,1,0:T(4,128)(2,1)}, u32[]{:S(2)}, u32[]{:S(2)}) async-start(bf16[16,3,4096]{2,1,0:T(4,128)(2,1)} %bitcast.91), calls=%async_computation | async-start | bytes 1048576 | tf_op jit(solution)/shard_map/while/body/eval_jaxpr/all_to_all | solution.py:97
  1539.2 7.5 collective-permute-start
  1549.0 21.4 %all-to-all-start = ((bf16[16,3,4096]{2,1,0:T(4,128)(2,1)}), bf16[16,3,4096]{2,1,0:T(4,128)(2,1)}, u32[]{:S(2)}, u32[]{:S(2)}) async-start(bf16[16,3,4096]{2,1,0:T(4,128)(2,1)} %bitcast.91), calls=%async_computation | async-start | bytes 1048576 | tf_op jit(solution)/shard_map/while/body/eval_jaxpr/all_to_all | solution.py:97
  1600.0 7.6 collective-permute-start
  1609.8 21.4 %all-to-all-start = ((bf16[16,3,4096]{2,1,0:T(4,128)(2,1)}), bf16[16,3,4096]{2,1,0:T(4,128)(2,1)}, u32[]{:S(2)}, u32[]{:S(2)}) async-start(bf16[16,3,4096]{2,1,0:T(4,128)(2,1)} %bitcast.91), calls=%async_computation | async-start | bytes 1048576 | tf_op jit(solution)/shard_map/while/body/eval_jaxpr/all_to_all | solution.py:97
  1660.8 7.5 collective-permute-start
  1670.6 21.4 %all-to-all-start = ((bf16[16,3,4096]{2,1,0:T(4,128)(2,1)}), bf16[16,3,4096]{2,1,0:T(4,128)(2,1)}, u32[]{:S(2)}, u32[]{:S(2)}) async-start(bf16[16,3,4096]{2,1,0:T(4,128)(2,1)} %bitcast.91), calls=%async_computation | async-start | bytes 1048576 | tf_op jit(solution)/shard_map/while/body/eval_jaxpr/all_to_all | solution.py:97
  1721.5 7.6 collective-permute-start
  1731.3 21.4 %all-to-all-start = ((bf16[16,3,4096]{2,1,0:T(4,128)(2,1)}), bf16[16,3,4096]{2,1,0:T(4,128)(2,1)}, u32[]{:S(2)}, u32[]{:S(2)}) async-start(bf16[16,3,4096]{2,1,0:T(4,128)(2,1)} %bitcast.91), calls=%async_computation | async-start | bytes 1048576 | tf_op jit(solution)/shard_map/while/body/eval_jaxpr/all_to_all | solution.py:97
  1782.3 7.6 collective-permute-start
  1792.1 21.4 %all-to-all-start = ((bf16[16,3,4096]{2,1,0:T(4,128)(2,1)}), bf16[16,3,4096]{2,1,0:T(4,128)(2,1)}, u32[]{:S(2)}, u32[]{:S(2)}) async-start(bf16[16,3,4096]{2,1,0:T(4,128)(2,1)} %bitcast.91), calls=%async_computation | async-start | bytes 1048576 | tf_op jit(solution)/shard_map/while/body/eval_jaxpr/all_to_all | solution.py:97
  1843.1 7.5 collective-permute-start
  1852.9 21.4 %all-to-all-start = ((bf16[16,3,4096]{2,1,0:T(4,128)(2,1)}), bf16[16,3,4096]{2,1,0:T(4,128)(2,1)}, u32[]{:S(2)}, u32[]{:S(2)}) async-start(bf16[16,3,4096]{2,1,0:T(4,128)(2,1)} %bitcast.91), calls=%async_computation | async-start | bytes 1048576 | tf_op jit(solution)/shard_map/while/body/eval_jaxpr/all_to_all | solution.py:97
  1903.8 7.6 collective-permute-start
  1913.7 21.4 %all-to-all-start = ((bf16[16,3,4096]{2,1,0:T(4,128)(2,1)}), bf16[16,3,4096]{2,1,0:T(4,128)(2,1)}, u32[]{:S(2)}, u32[]{:S(2)}) async-start(bf16[16,3,4096]{2,1,0:T(4,128)(2,1)} %bitcast.91), calls=%async_computation | async-start | bytes 1048576 | tf_op jit(solution)/shard_map/while/body/eval_jaxpr/all_to_all | solution.py:97
  1964.6 7.6 collective-permute-start
  1974.4 21.4 %all-to-all-start = ((bf16[16,3,4096]{2,1,0:T(4,128)(2,1)}), bf16[16,3,4096]{2,1,0:T(4,128)(2,1)}, u32[]{:S(2)}, u32[]{:S(2)}) async-start(bf16[16,3,4096]{2,1,0:T(4,128)(2,1)} %bitcast.91), calls=%async_computation | async-start | bytes 1048576 | tf_op jit(solution)/shard_map/while/body/eval_jaxpr/all_to_all | solution.py:97
  2025.4 5.2 collective-permute-start
  (130 other events, 2464.0 us)
where the time goes:
time: 2040 us; the launch traced here: 2030 us
  waiting for transfers between devices  909 us (45%)
  blocking collectives  630 us (31%)
  starting transfers between devices  180 us (9%)
  matrix products  160 us (8%)
  local copies, waits for them, and re-layouts  137 us (7%)
    all_to_all x31, blocking collectives, tick(): lax.all_to_all(back.reshape(expert_count, capacity, model_width), 'expert...  630 us
    all_to_all x31, waiting for transfers between devices, tick(): lax.all_to_all(grad_rows, 'expert', split_axis=0, concat_axis=0, tiled=True)  534 us
    ppermute x31, waiting for transfers between devices, passed_along(): return lax.ppermute(x, axis, pairs)  237 us
    all_to_all x1, waiting for transfers between devices, on_device(): lax.all_to_all(outgoing, 'expert', split_axis=1, concat_axis=1, tiled=True)  138 us
    all_to_all x31, starting transfers between devices, tick(): lax.all_to_all(grad_rows, 'expert', split_axis=0, concat_axis=0, tiled=True)  130 us
    dot_general x31, matrix products, tick(): jnp.einsum('tec,ekcd->td', combine_micro, returned, preferred_element_typ...  56.5 us
  transfers between devices with their start and end apart: 63, of which 63 were waited for; matrix products, arithmetic and copies ran while one was open for 0% of the time, Pallas kernels for 0%

commit v1 on v0

--- a/solution.py
+++ b/solution.py
@@ -69,7 +69,12 @@
     outgoing = spread(
         jnp.einsum("mtec,mtd->mecd", dispatch, inputs, preferred_element_type=jnp.float32)
     )
-    received = lax.all_to_all(outgoing, "expert", split_axis=1, concat_axis=1, tiled=True)
+    received = jnp.concatenate(
+        lax.all_to_all(
+            jnp.stack(jnp.split(outgoing, lax.axis_size("expert"), axis=1)), "expert", 0, 0
+        ),
+        axis=1,
+    )
     item_count = received.shape[0]
     row_block = received.reshape(-1, model_width)
     pre_gate = jnp.dot(row_block, gate_slice, preferred_element_type=jnp.float32)

time: 2040 us -> 2050 us (level)
  no operation moved by 1% of the time
where the time goes in v1:
time: 2050 us; the launch traced here: 2040 us
  waiting for transfers between devices  909 us (44%)
  blocking collectives  625 us (30%)
  starting transfers between devices  179 us (9%)
  matrix products  174 us (8%)
  local copies, waits for them, and re-layouts  134 us (7%)
    all_to_all x31, blocking collectives, tick(): lax.all_to_all(back.reshape(expert_count, capacity, model_width), 'expert...  625 us
    all_to_all x31, waiting for transfers between devices, tick(): lax.all_to_all(grad_rows, 'expert', split_axis=0, concat_axis=0, tiled=True)  534 us
    ppermute x31, waiting for transfers between devices, passed_along(): return lax.ppermute(x, axis, pairs)  237 us
    all_to_all x1, waiting for transfers between devices, on_device(): lax.all_to_all(jnp.stack(jnp.split(outgoing, lax.axis_size('expert'), axi...  138 us
    all_to_all x31, starting transfers between devices, tick(): lax.all_to_all(grad_rows, 'expert', split_axis=0, concat_axis=0, tiled=True)  130 us
    dot_general x31, matrix products, tick(): jnp.einsum('tec,ekcd->td', combine_micro, returned, preferred_element_typ...  56.5 us
  transfers between devices with their start and end apart: 63, of which 63 were waited for; matrix products, arithmetic and copies ran while one was open for 0% of the time, Pallas kernels for 0%

profile of v1, /device:TPU:1, one launch (start us, length us, event | category | flops | bytes accessed | tf_op | source)
XLA Modules:
  0.0 2036.5 jit_solution(7968287910833695247)
XLA Ops:
  30.8 137.7 %all-to-all-done.2 = bf16[16,16,1,3,4096]{4,1,3,2,0:T(8,128)(2,1)} async-done(((bf16[16,16,1,3,4096]{4,1,3,2,0:T(8,128)(2,1)}), bf16[16,16,1,3,4096]{4,1,3,2,0:T(8,128)(2,1)}, u32[]{:S(2)}, u32[]{:S(2)}) %all-to-all-start.2) | async-done | bytes 6291488 | tf_op jit(solution)/shard_map/all_to_all | solution.py:73
  203.3 1833.2 %while.17 = (s32[]{:T(128)}, bf16[8,4096]{1,0:T(8,128)(2,1)S(1)}, bf16[16,8,4096]{2,1,0:T(8,128)(2,1)}, pred[]{:T(512)}, s32[]{:T(128)}, /*index=5*/bf16[16,8,40...) while((s32[]{:T(128)}, bf16[8,4096]{1,0:T(8,128)(2,1)S(1)}, ...), condition=%wide.region_8.9_spmd, body=%wide.region_4.8_spmd.sunk | while | flops 306167808 | bytes 24051140 | solution.py:136
  211.3 17.4 all-to-all-done
  229.8 20.2 all_to_all.29
  263.7 17.5 all-to-all-done
  282.2 20.2 all_to_all.29
  316.2 17.5 all-to-all-done
  334.7 20.2 all_to_all.29
  368.6 17.5 all-to-all-done
  387.2 20.2 all_to_all.29
  421.1 17.3 all-to-all-done
  439.5 20.2 all_to_all.29
  475.6 17.2 all-to-all-done
  493.9 20.2 all_to_all.29
  530.2 17.2 all-to-all-done
  548.5 20.2 all_to_all.29
  584.8 17.2 all-to-all-done
  603.1 20.2 all_to_all.29
  639.4 17.2 all-to-all-done
  657.6 20.2 all_to_all.29
  712.2 20.2 all_to_all.29
  748.5 17.2 all-to-all-done
  766.8 20.2 all_to_all.29
  803.1 17.2 all-to-all-done
  821.4 20.2 all_to_all.29
  857.7 17.2 all-to-all-done
  876.0 20.2 all_to_all.29
  912.3 17.2 all-to-all-done
  930.6 20.2 all_to_all.29
  966.9 17.2 all-to-all-done
  985.1 20.2 all_to_all.29
  1008.8 60.7 %collective-permute-done = bf16[8,4096]{1,0:T(8,128)(2,1)S(1)} collective-permute-done((bf16[8,4096]{1,0:T(8,128)(2,1)S(1)}, bf16[8,4096]{1,0:T(8,128)(2,1)S(1)}, u32[]{:S(2)}, u32[]{:S(2)}) %collective-permute-start) | collective-permute-done | bytes 65568 | tf_op jit(solution)/shard_map/while/body/eval_jaxpr/ppermute | solution.py:13
  1075.9 17.2 all-to-all-done
  1100.2 20.2 all_to_all.29
  1136.5 17.2 all-to-all-done
  1160.7 20.2 all_to_all.29
  1197.1 17.2 all-to-all-done
  1221.3 20.2 all_to_all.29
  1257.6 17.2 all-to-all-done
  1281.9 20.2 all_to_all.29
  1318.2 17.2 all-to-all-done
  1342.5 20.2 all_to_all.29
  1378.8 17.2 all-to-all-done
  1403.1 20.2 all_to_all.29
  1439.4 17.2 all-to-all-done
  1463.7 20.2 all_to_all.29
  1500.0 17.2 all-to-all-done
  1524.3 20.2 all_to_all.29
  1560.6 17.2 all-to-all-done
  1584.9 20.2 all_to_all.29
  1621.2 17.2 all-to-all-done
  1645.5 20.2 all_to_all.29
  1681.8 17.2 all-to-all-done
  1706.0 20.2 all_to_all.29
  1742.4 17.2 all-to-all-done
  1766.6 20.2 all_to_all.29
  1802.9 17.2 all-to-all-done
  1827.2 20.2 all_to_all.29
  1863.5 17.2 all-to-all-done
  1887.8 20.2 all_to_all.29
  1924.1 17.2 all-to-all-done
  1948.4 20.2 all_to_all.29
  1984.7 17.2 all-to-all-done
  2009.0 20.2 all_to_all.29
  (530 shorter events, 789.8 us)
Async XLA Ops:
  19.8 148.7 %all-to-all-start.2 = ((bf16[16,16,1,3,4096]{4,1,3,2,0:T(8,128)(2,1)}), bf16[16,16,1,3,4096]{4,1,3,2,0:T(8,128)(2,1)}, u32[]{:S(2)}, u32[]{:S(2)}) async-start(bf16[16,16,1,3,4096]{4,1,3,2,0:T(8,128)(2,1)} %fusion.22), calls=%async_computation.2 | async-start | bytes 12582912 | tf_op jit(solution)/shard_map/all_to_all | solution.py:73
  203.5 25.2 %copy-start.6 = (bf16[8,4096]{1,0:T(8,128)(2,1)}, bf16[8,4096]{1,0:T(8,128)(2,1)S(1)}, u32[]{:S(2)}) copy-start(bf16[8,4096]{1,0:T(8,128)(2,1)S(1)} %get-tuple-element.461) | copy-start | bytes 196612 | tf_op jit(solution)/shard_map/while
  205.8 22.9 %all-to-all-start = ((bf16[16,3,4096]{2,1,0:T(4,128)(2,1)}), bf16[16,3,4096]{2,1,0:T(4,128)(2,1)}, u32[]{:S(2)}, u32[]{:S(2)}) async-start(bf16[16,3,4096]{2,1,0:T(4,128)(2,1)} %bitcast.158), calls=%async_computation | async-start | bytes 1048576 | tf_op jit(solution)/shard_map/while/body/eval_jaxpr/all_to_all | solution.py:102
  252.1 5.2 collective-permute-start
  259.5 21.6 %all-to-all-start = ((bf16[16,3,4096]{2,1,0:T(4,128)(2,1)}), bf16[16,3,4096]{2,1,0:T(4,128)(2,1)}, u32[]{:S(2)}, u32[]{:S(2)}) async-start(bf16[16,3,4096]{2,1,0:T(4,128)(2,1)} %bitcast.158), calls=%async_computation | async-start | bytes 1048576 | tf_op jit(solution)/shard_map/while/body/eval_jaxpr/all_to_all | solution.py:102
  304.5 5.2 collective-permute-start
  312.0 21.6 %all-to-all-start = ((bf16[16,3,4096]{2,1,0:T(4,128)(2,1)}), bf16[16,3,4096]{2,1,0:T(4,128)(2,1)}, u32[]{:S(2)}, u32[]{:S(2)}) async-start(bf16[16,3,4096]{2,1,0:T(4,128)(2,1)} %bitcast.158), calls=%async_computation | async-start | bytes 1048576 | tf_op jit(solution)/shard_map/while/body/eval_jaxpr/all_to_all | solution.py:102
  357.0 5.2 collective-permute-start
  364.4 21.6 %all-to-all-start = ((bf16[16,3,4096]{2,1,0:T(4,128)(2,1)}), bf16[16,3,4096]{2,1,0:T(4,128)(2,1)}, u32[]{:S(2)}, u32[]{:S(2)}) async-start(bf16[16,3,4096]{2,1,0:T(4,128)(2,1)} %bitcast.158), calls=%async_computation | async-start | bytes 1048576 | tf_op jit(solution)/shard_map/while/body/eval_jaxpr/all_to_all | solution.py:102
  409.5 5.2 collective-permute-start
  416.9 21.5 %all-to-all-start = ((bf16[16,3,4096]{2,1,0:T(4,128)(2,1)}), bf16[16,3,4096]{2,1,0:T(4,128)(2,1)}, u32[]{:S(2)}, u32[]{:S(2)}) async-start(bf16[16,3,4096]{2,1,0:T(4,128)(2,1)} %bitcast.158), calls=%async_computation | async-start | bytes 1048576 | tf_op jit(solution)/shard_map/while/body/eval_jaxpr/all_to_all | solution.py:102
  461.8 7.4 collective-permute-start
  471.5 21.4 %all-to-all-start = ((bf16[16,3,4096]{2,1,0:T(4,128)(2,1)}), bf16[16,3,4096]{2,1,0:T(4,128)(2,1)}, u32[]{:S(2)}, u32[]{:S(2)}) async-start(bf16[16,3,4096]{2,1,0:T(4,128)(2,1)} %bitcast.158), calls=%async_computation | async-start | bytes 1048576 | tf_op jit(solution)/shard_map/while/body/eval_jaxpr/all_to_all | solution.py:102
  516.2 7.6 collective-permute-start
  526.1 21.4 %all-to-all-start = ((bf16[16,3,4096]{2,1,0:T(4,128)(2,1)}), bf16[16,3,4096]{2,1,0:T(4,128)(2,1)}, u32[]{:S(2)}, u32[]{:S(2)}) async-start(bf16[16,3,4096]{2,1,0:T(4,128)(2,1)} %bitcast.158), calls=%async_computation | async-start | bytes 1048576 | tf_op jit(solution)/shard_map/while/body/eval_jaxpr/all_to_all | solution.py:102
  570.8 7.6 collective-permute-start
  580.6 21.4 %all-to-all-start = ((bf16[16,3,4096]{2,1,0:T(4,128)(2,1)}), bf16[16,3,4096]{2,1,0:T(4,128)(2,1)}, u32[]{:S(2)}, u32[]{:S(2)}) async-start(bf16[16,3,4096]{2,1,0:T(4,128)(2,1)} %bitcast.158), calls=%async_computation | async-start | bytes 1048576 | tf_op jit(solution)/shard_map/while/body/eval_jaxpr/all_to_all | solution.py:102
  625.4 7.6 collective-permute-start
  635.2 21.4 %all-to-all-start = ((bf16[16,3,4096]{2,1,0:T(4,128)(2,1)}), bf16[16,3,4096]{2,1,0:T(4,128)(2,1)}, u32[]{:S(2)}, u32[]{:S(2)}) async-start(bf16[16,3,4096]{2,1,0:T(4,128)(2,1)} %bitcast.158), calls=%async_computation | async-start | bytes 1048576 | tf_op jit(solution)/shard_map/while/body/eval_jaxpr/all_to_all | solution.py:102
  680.0 7.6 collective-permute-start
  689.8 21.4 %all-to-all-start = ((bf16[16,3,4096]{2,1,0:T(4,128)(2,1)}), bf16[16,3,4096]{2,1,0:T(4,128)(2,1)}, u32[]{:S(2)}, u32[]{:S(2)}) async-start(bf16[16,3,4096]{2,1,0:T(4,128)(2,1)} %bitcast.158), calls=%async_computation | async-start | bytes 1048576 | tf_op jit(solution)/shard_map/while/body/eval_jaxpr/all_to_all | solution.py:102
  734.6 7.6 collective-permute-start
  744.4 21.4 %all-to-all-start = ((bf16[16,3,4096]{2,1,0:T(4,128)(2,1)}), bf16[16,3,4096]{2,1,0:T(4,128)(2,1)}, u32[]{:S(2)}, u32[]{:S(2)}) async-start(bf16[16,3,4096]{2,1,0:T(4,128)(2,1)} %bitcast.158), calls=%async_computation | async-start | bytes 1048576 | tf_op jit(solution)/shard_map/while/body/eval_jaxpr/all_to_all | solution.py:102
  789.1 7.6 collective-permute-start
  799.0 21.4 %all-to-all-start = ((bf16[16,3,4096]{2,1,0:T(4,128)(2,1)}), bf16[16,3,4096]{2,1,0:T(4,128)(2,1)}, u32[]{:S(2)}, u32[]{:S(2)}) async-start(bf16[16,3,4096]{2,1,0:T(4,128)(2,1)} %bitcast.158), calls=%async_computation | async-start | bytes 1048576 | tf_op jit(solution)/shard_map/while/body/eval_jaxpr/all_to_all | solution.py:102
  843.7 7.6 collective-permute-start
  853.6 21.4 %all-to-all-start = ((bf16[16,3,4096]{2,1,0:T(4,128)(2,1)}), bf16[16,3,4096]{2,1,0:T(4,128)(2,1)}, u32[]{:S(2)}, u32[]{:S(2)}) async-start(bf16[16,3,4096]{2,1,0:T(4,128)(2,1)} %bitcast.158), calls=%async_computation | async-start | bytes 1048576 | tf_op jit(solution)/shard_map/while/body/eval_jaxpr/all_to_all | solution.py:102
  898.3 7.6 collective-permute-start
  908.1 21.4 %all-to-all-start = ((bf16[16,3,4096]{2,1,0:T(4,128)(2,1)}), bf16[16,3,4096]{2,1,0:T(4,128)(2,1)}, u32[]{:S(2)}, u32[]{:S(2)}) async-start(bf16[16,3,4096]{2,1,0:T(4,128)(2,1)} %bitcast.158), calls=%async_computation | async-start | bytes 1048576 | tf_op jit(solution)/shard_map/while/body/eval_jaxpr/all_to_all | solution.py:102
  952.9 7.6 collective-permute-start
  962.7 21.4 %all-to-all-start = ((bf16[16,3,4096]{2,1,0:T(4,128)(2,1)}), bf16[16,3,4096]{2,1,0:T(4,128)(2,1)}, u32[]{:S(2)}, u32[]{:S(2)}) async-start(bf16[16,3,4096]{2,1,0:T(4,128)(2,1)} %bitcast.158), calls=%async_computation | async-start | bytes 1048576 | tf_op jit(solution)/shard_map/while/body/eval_jaxpr/all_to_all | solution.py:102
  1007.5 62.0 %collective-permute-start = (bf16[8,4096]{1,0:T(8,128)(2,1)S(1)}, bf16[8,4096]{1,0:T(8,128)(2,1)S(1)}, u32[]{:S(2)}, u32[]{:S(2)}) collective-permute-start(bf16[8,4096]{1,0:T(8,128)(2,1)S(1)} %get-tuple-element.441), channel_id=1, source_target_pairs={{16,0},{32,16},{48,32},{64,48},{80,64},{96,80},{112,96},{128,112},... | collective-permute-start | bytes 196616 | tf_op jit(solution)/shard_map/while/body/eval_jaxpr/ppermute | solution.py:13
  1071.7 21.4 %all-to-all-start = ((bf16[16,3,4096]{2,1,0:T(4,128)(2,1)}), bf16[16,3,4096]{2,1,0:T(4,128)(2,1)}, u32[]{:S(2)}, u32[]{:S(2)}) async-start(bf16[16,3,4096]{2,1,0:T(4,128)(2,1)} %bitcast.158), calls=%async_computation | async-start | bytes 1048576 | tf_op jit(solution)/shard_map/while/body/eval_jaxpr/all_to_all | solution.py:102
  1122.5 7.6 collective-permute-start
  1132.3 21.4 %all-to-all-start = ((bf16[16,3,4096]{2,1,0:T(4,128)(2,1)}), bf16[16,3,4096]{2,1,0:T(4,128)(2,1)}, u32[]{:S(2)}, u32[]{:S(2)}) async-start(bf16[16,3,4096]{2,1,0:T(4,128)(2,1)} %bitcast.158), calls=%async_computation | async-start | bytes 1048576 | tf_op jit(solution)/shard_map/while/body/eval_jaxpr/all_to_all | solution.py:102
  1183.1 7.6 collective-permute-start
  1192.9 21.4 %all-to-all-start = ((bf16[16,3,4096]{2,1,0:T(4,128)(2,1)}), bf16[16,3,4096]{2,1,0:T(4,128)(2,1)}, u32[]{:S(2)}, u32[]{:S(2)}) async-start(bf16[16,3,4096]{2,1,0:T(4,128)(2,1)} %bitcast.158), calls=%async_computation | async-start | bytes 1048576 | tf_op jit(solution)/shard_map/while/body/eval_jaxpr/all_to_all | solution.py:102
  1243.7 7.6 collective-permute-start
  1253.5 21.4 %all-to-all-start = ((bf16[16,3,4096]{2,1,0:T(4,128)(2,1)}), bf16[16,3,4096]{2,1,0:T(4,128)(2,1)}, u32[]{:S(2)}, u32[]{:S(2)}) async-start(bf16[16,3,4096]{2,1,0:T(4,128)(2,1)} %bitcast.158), calls=%async_computation | async-start | bytes 1048576 | tf_op jit(solution)/shard_map/while/body/eval_jaxpr/all_to_all | solution.py:102
  1304.2 7.6 collective-permute-start
  1314.1 21.4 %all-to-all-start = ((bf16[16,3,4096]{2,1,0:T(4,128)(2,1)}), bf16[16,3,4096]{2,1,0:T(4,128)(2,1)}, u32[]{:S(2)}, u32[]{:S(2)}) async-start(bf16[16,3,4096]{2,1,0:T(4,128)(2,1)} %bitcast.158), calls=%async_computation | async-start | bytes 1048576 | tf_op jit(solution)/shard_map/while/body/eval_jaxpr/all_to_all | solution.py:102
  1364.8 7.6 collective-permute-start
  1374.7 21.4 %all-to-all-start = ((bf16[16,3,4096]{2,1,0:T(4,128)(2,1)}), bf16[16,3,4096]{2,1,0:T(4,128)(2,1)}, u32[]{:S(2)}, u32[]{:S(2)}) async-start(bf16[16,3,4096]{2,1,0:T(4,128)(2,1)} %bitcast.158), calls=%async_computation | async-start | bytes 1048576 | tf_op jit(solution)/shard_map/while/body/eval_jaxpr/all_to_all | solution.py:102
  1425.4 7.6 collective-permute-start
  1435.3 21.4 %all-to-all-start = ((bf16[16,3,4096]{2,1,0:T(4,128)(2,1)}), bf16[16,3,4096]{2,1,0:T(4,128)(2,1)}, u32[]{:S(2)}, u32[]{:S(2)}) async-start(bf16[16,3,4096]{2,1,0:T(4,128)(2,1)} %bitcast.158), calls=%async_computation | async-start | bytes 1048576 | tf_op jit(solution)/shard_map/while/body/eval_jaxpr/all_to_all | solution.py:102
  1486.0 7.6 collective-permute-start
  1495.8 21.4 %all-to-all-start = ((bf16[16,3,4096]{2,1,0:T(4,128)(2,1)}), bf16[16,3,4096]{2,1,0:T(4,128)(2,1)}, u32[]{:S(2)}, u32[]{:S(2)}) async-start(bf16[16,3,4096]{2,1,0:T(4,128)(2,1)} %bitcast.158), calls=%async_computation | async-start | bytes 1048576 | tf_op jit(solution)/shard_map/while/body/eval_jaxpr/all_to_all | solution.py:102
  1546.6 7.6 collective-permute-start
  1556.4 21.4 %all-to-all-start = ((bf16[16,3,4096]{2,1,0:T(4,128)(2,1)}), bf16[16,3,4096]{2,1,0:T(4,128)(2,1)}, u32[]{:S(2)}, u32[]{:S(2)}) async-start(bf16[16,3,4096]{2,1,0:T(4,128)(2,1)} %bitcast.158), calls=%async_computation | async-start | bytes 1048576 | tf_op jit(solution)/shard_map/while/body/eval_jaxpr/all_to_all | solution.py:102
  1607.2 7.6 collective-permute-start
  1617.0 21.4 %all-to-all-start = ((bf16[16,3,4096]{2,1,0:T(4,128)(2,1)}), bf16[16,3,4096]{2,1,0:T(4,128)(2,1)}, u32[]{:S(2)}, u32[]{:S(2)}) async-start(bf16[16,3,4096]{2,1,0:T(4,128)(2,1)} %bitcast.158), calls=%async_computation | async-start | bytes 1048576 | tf_op jit(solution)/shard_map/while/body/eval_jaxpr/all_to_all | solution.py:102
  1667.8 7.6 collective-permute-start
  1677.6 21.4 %all-to-all-start = ((bf16[16,3,4096]{2,1,0:T(4,128)(2,1)}), bf16[16,3,4096]{2,1,0:T(4,128)(2,1)}, u32[]{:S(2)}, u32[]{:S(2)}) async-start(bf16[16,3,4096]{2,1,0:T(4,128)(2,1)} %bitcast.158), calls=%async_computation | async-start | bytes 1048576 | tf_op jit(solution)/shard_map/while/body/eval_jaxpr/all_to_all | solution.py:102
  1728.4 7.6 collective-permute-start
  1738.2 21.4 %all-to-all-start = ((bf16[16,3,4096]{2,1,0:T(4,128)(2,1)}), bf16[16,3,4096]{2,1,0:T(4,128)(2,1)}, u32[]{:S(2)}, u32[]{:S(2)}) async-start(bf16[16,3,4096]{2,1,0:T(4,128)(2,1)} %bitcast.158), calls=%async_computation | async-start | bytes 1048576 | tf_op jit(solution)/shard_map/while/body/eval_jaxpr/all_to_all | solution.py:102
  1789.0 7.6 collective-permute-start
  1798.8 21.4 %all-to-all-start = ((bf16[16,3,4096]{2,1,0:T(4,128)(2,1)}), bf16[16,3,4096]{2,1,0:T(4,128)(2,1)}, u32[]{:S(2)}, u32[]{:S(2)}) async-start(bf16[16,3,4096]{2,1,0:T(4,128)(2,1)} %bitcast.158), calls=%async_computation | async-start | bytes 1048576 | tf_op jit(solution)/shard_map/while/body/eval_jaxpr/all_to_all | solution.py:102
  1849.5 7.6 collective-permute-start
  1859.4 21.4 %all-to-all-start = ((bf16[16,3,4096]{2,1,0:T(4,128)(2,1)}), bf16[16,3,4096]{2,1,0:T(4,128)(2,1)}, u32[]{:S(2)}, u32[]{:S(2)}) async-start(bf16[16,3,4096]{2,1,0:T(4,128)(2,1)} %bitcast.158), calls=%async_computation | async-start | bytes 1048576 | tf_op jit(solution)/shard_map/while/body/eval_jaxpr/all_to_all | solution.py:102
  1910.1 7.6 collective-permute-start
  1920.0 21.4 %all-to-all-start = ((bf16[16,3,4096]{2,1,0:T(4,128)(2,1)}), bf16[16,3,4096]{2,1,0:T(4,128)(2,1)}, u32[]{:S(2)}, u32[]{:S(2)}) async-start(bf16[16,3,4096]{2,1,0:T(4,128)(2,1)} %bitcast.158), calls=%async_computation | async-start | bytes 1048576 | tf_op jit(solution)/shard_map/while/body/eval_jaxpr/all_to_all | solution.py:102
  1970.7 7.6 collective-permute-start
  1980.6 21.4 %all-to-all-start = ((bf16[16,3,4096]{2,1,0:T(4,128)(2,1)}), bf16[16,3,4096]{2,1,0:T(4,128)(2,1)}, u32[]{:S(2)}, u32[]{:S(2)}) async-start(bf16[16,3,4096]{2,1,0:T(4,128)(2,1)} %bitcast.158), calls=%async_computation | async-start | bytes 1048576 | tf_op jit(solution)/shard_map/while/body/eval_jaxpr/all_to_all | solution.py:102
  2031.3 5.2 collective-permute-start
  (52 other events, 801.5 us)
